TPU v7x, 32 devices: a whole 2x2x4 slice. The times are simulated.
32 devices in a mesh: wide: 16 (over z, x, core), tm: 2 (over y).
Axes of the slice: x: 2, y: 2, z: 4, core: 2. Of those that a mesh axis runs over, the one named last changes fastest.
Arguments:
- voltages: int32 [256, 131072], P('wide', 'tm'), may hold values from -128 to 127
- taps: int32 [16, 1024], replicated, may hold values from -32 to 32
Outputs:
- visibility: float32 [256, 2, 512, 256], P('tm', None, 'wide')
All inputs are finite; a program needn't handle non-finite values.
Results may differ from a plain program's by a relative error of at most 0.0024.
Values may be sent and summed in bfloat16 or wider, within the bound.
A program may use at most 64 MiB of HBM per device.

v0:
```python
import jax
import jax.numpy as jnp
from jax import lax
from jax.sharding import PartitionSpec as P

FIR_SCALE = 2.0 ** (-12)


def shifted(array, axis, by):
    devices = lax.axis_size(axis)
    pairs = [(i, i + by) for i in range(devices) if 0 <= i + by < devices]
    return lax.ppermute(array, axis, pairs)


def gram_rows(own_rows, own_rotated, full_rows):
    real_part = jnp.einsum("akt,bkt->akb", own_rows, full_rows, preferred_element_type=jnp.float32)
    imag_part = jnp.einsum(
        "akt,bkt->akb", own_rotated, full_rows, preferred_element_type=jnp.float32
    )
    return jnp.stack([real_part, imag_part], axis=1)


def shards(voltages, taps):
    local_inputs = voltages.shape[0]
    length = taps.shape[1]
    lags = taps.shape[0]
    spectra_dev = voltages.shape[1] // length
    channels = length // 2
    frames = voltages.astype(jnp.bfloat16).reshape(local_inputs, spectra_dev, length)
    previous = shifted(frames[:, spectra_dev - (lags - 1) :, :], "tm", 1)
    extended = jnp.concatenate([previous, frames], axis=1).astype(jnp.float32)
    taps_float = taps.astype(jnp.float32)
    filtered = jnp.zeros((local_inputs, spectra_dev, length), jnp.float32)
    for lag in range(lags):
        filtered = (
            filtered
            + taps_float[lag] * extended[:, lags - 1 - lag : lags - 1 - lag + spectra_dev, :]
        )
    filtered = filtered * FIR_SCALE
    sample_idx = jnp.arange(length, dtype=jnp.int32)
    channel_idx = jnp.arange(channels, dtype=jnp.int32)
    phase_steps = sample_idx[:, None] * channel_idx[None, :] % length
    angles = 2.0 * jnp.pi / length * phase_steps.astype(jnp.float32)
    dft_table = jnp.stack([jnp.cos(angles), -jnp.sin(angles)], axis=1) * length ** (-0.5)
    spectra = jnp.einsum(
        "asl,lrc->acrs",
        filtered,
        dft_table,
        precision=lax.Precision.HIGHEST,
        preferred_element_type=jnp.float32,
    ).astype(jnp.bfloat16)
    widen = lax.axis_size("wide")
    ranks = lax.axis_size("tm")
    norm_factor = 1.0 / (spectra_dev * ranks)
    packed = spectra.reshape(local_inputs, widen, channels // widen, 2 * spectra_dev)
    arrived = lax.all_to_all(packed, "wide", split_axis=1, concat_axis=0, tiled=True)
    all_inputs = arrived.shape[0]
    local_channels = arrived.shape[2]
    split_parts = arrived.reshape(all_inputs, local_channels, 2, spectra_dev)
    own_count = all_inputs // ranks
    first_row = lax.axis_index("tm") * own_count
    segment = lax.all_gather(split_parts, "tm", axis=3, tiled=True)
    full_rows = jnp.concatenate([segment[:, :, 0, :], segment[:, :, 1, :]], axis=-1)
    rotated = jnp.concatenate([segment[:, :, 1, :], -segment[:, :, 0, :]], axis=-1)
    own_rows = lax.dynamic_slice_in_dim(full_rows, first_row, own_count, 0)
    own_rotated = lax.dynamic_slice_in_dim(rotated, first_row, own_count, 0)
    summed = gram_rows(own_rows, own_rotated, full_rows)
    return summed * norm_factor


def solution(mesh):
    placed = (P("wide", "tm"), P())
    return jax.shard_map(
        shards, mesh=mesh, in_specs=placed, out_specs=P("tm", None, "wide", None), check_vma=False
    )
```

profile of v0, /device:TPU:0, one launch (start us, length us, event | category | flops | bytes accessed | tf_op | source)
XLA Modules:
  0.0 233.2 jit_solution(13914360687842572392)
XLA Ops:
  6.5 2.4 %convert_element_type.33 = bf16[16,65536]{1,0:T(8,128)(2,1)S(1)} convert(s32[16,65536]{1,0:T(8,128)} %param.2) | non-fusion elementwise | flops 1048576 | bytes 6291456 | tf_op jit(solution)/shard_map/convert_element_type | solution.py:29
  8.9 1.2 copy.17
  10.1 0.1 slice.143
  10.3 4.9 %collective-permute-start = (bf16[16,15,1024]{2,1,0:T(8,128)(2,1)S(1)}, bf16[16,15,1024]{2,1,0:T(8,128)(2,1)S(1)}, u32[]{:S(2)}, u32[]{:S(2)}) collective-permute-start(bf16[16,15,1024]{2,1,0:T(8,128)(2,1)S(1)} %slice.143), channel_id=1, source_target_pairs={{0,1},{2,3},{4,5},{6,7},{8,9},{10,11},{12,13},{14,15},{16,17},{18,... | collective-permute-start | bytes 1474568 | tf_op jit(solution)/shard_map/ppermute | solution.py:12
  15.2 9.2 %sine_negate_fusion = (f32[1024,1,512]{2,0,1:T(8,128)}, f32[1024,1,512]{2,0,1:T(8,128)}) fusion(), kind=kLoop, calls=%fused_computation.76 | loop fusion | flops 7864320 | bytes 4194304 | tf_op jit(solution)/shard_map/neg | solution.py:44
  24.5 1.8 collective-permute-done
  26.3 0.8 maximum_convert_fusion
  27.1 24.9 %convert_bitcast_fusion = bf16[16,512,2,64]{1,3,0,2:T(8,128)(2,1)} fusion(f32[16,79,1024]{2,1,0:T(8,128)S(1)} %maximum_convert_fusion, f32[1024]{0:T(1024)S(1)} %bitcast.59, f32[1024]{0:T(1024)S(1)} %bitcast.60, f32[1024]{0:T(1024)S(1)} %bitcast.61, f32[1024]{0:T(1024)S(1)} %bitcast.62, f32[1024]{0:T(1024)S(1)} %bitcast.63, f32[1024]{0:T(1024)S(1)} %bitcast.64, ...), kind=kOutput, calls=%fused_computation.57 | convolution fusion | flops 12921602048 | bytes 73465856 | tf_op jit(solution)/shard_map/asl,lrc->acrs/dot_general | solution.py:45
  52.0 10.7 %copy.8 = bf16[16,512,2,64]{3,2,1,0:T(2,128)(2,1)} copy(bf16[16,512,2,64]{1,3,0,2:T(8,128)(2,1)} %convert_bitcast_fusion) | data formatting | bytes 4194304 | tf_op jit(solution)/shard_map/convert_element_type | solution.py:51
  62.8 7.0 %reshape.96 = bf16[16,16,32,128]{3,2,1,0:T(8,128)(2,1)S(1)} reshape(bf16[16,512,2,64]{3,2,1,0:T(2,128)(2,1)} %copy.8) | data formatting | bytes 4194304 | tf_op jit(solution)/shard_map/reshape | solution.py:55
  69.8 0.5 copy.9
  70.4 53.0 %all_to_all.15 = bf16[16,16,32,128]{3,2,0,1:T(8,128)(2,1)S(1)} all-to-all(bf16[16,16,32,128]{3,2,0,1:T(8,128)(2,1)S(1)} %copy.9), channel_id=1, replica_groups=mesh['wide'=16,'tm'=2] {'wide'}, dimensions={1} | all-to-all | bytes 4194304 | tf_op jit(solution)/shard_map/all_to_all | solution.py:56
  123.4 3.2 %reshape.97 = bf16[256,32,2,64]{3,2,1,0:T(2,128)(2,1)} reshape(bf16[16,16,1,32,128]{4,3,1,0,2:T(8,128)(2,1)S(1)} %bitcast.52) | data formatting | bytes 4194304 | tf_op jit(solution)/shard_map/reshape | solution.py:59
  126.6 8.2 %copy.10 = bf16[256,32,2,64]{0,1,2,3:T(8,128)(2,1)} copy(bf16[256,32,2,64]{3,2,1,0:T(2,128)(2,1)} %reshape.97) | data formatting | bytes 4194304 | tf_op jit(solution)/shard_map/reshape | solution.py:59
  134.9 0.0 all-gather.2.cloned.1.call-update
  134.9 58.3 %all-gather.2.cloned.1.call-done = bf16[256,32,2,128]{0,1,2,3:T(8,128)(2,1)} async-done(((bf16[256,32,2,64]{0,1,2,3:T(8,128)(2,1)}), bf16[256,32,2,128]{0,1,2,3:T(8,128)(2,1)}) %all-gather.2.cloned.1.call-update) | async-done | bytes 4194320 | tf_op jit(solution)/shard_map/all_gather | solution.py:62
  193.2 4.7 %fusion.81 = (bf16[256,32,1,128]{0,1,2,3:T(8,128)(2,1)}, bf16[256,32,1,128]{0,1,2,3:T(8,128)(2,1)}) fusion(bf16[256,32,2,128]{0,1,2,3:T(8,128)(2,1)} %all-gather.2.cloned.1.call-done), kind=kLoop, calls=%fused_computation.89 | loop fusion | bytes 8388608 | tf_op jit(solution)/shard_map/slice | solution.py:63
  197.9 3.4 %copy.15 = bf16[256,32,1,128]{3,0,1,2:T(8,128)(2,1)S(1)} copy(bf16[256,32,1,128]{0,1,2,3:T(8,128)(2,1)} %get-tuple-element.5) | data formatting | bytes 4194304
  201.4 1.6 bitcast_negate_fusion
  203.0 4.5 %copy.16 = bf16[256,32,1,128]{3,0,1,2:T(8,128)(2,1)} copy(bf16[256,32,1,128]{0,1,2,3:T(8,128)(2,1)} %get-tuple-element.6) | data formatting | bytes 4194304
  207.5 3.3 %fusion.40 = f32[128,1,32,256]{0,3,2,1:T(8,128)S(1)} fusion(bf16[256,32,128]{2,0,1:T(8,128)(2,1)} %bitcast.56, bf16[256,32,128]{2,0,1:T(8,128)(2,1)S(1)} %bitcast.54, s32[]{:T(128)S(6)} %select_n.25), kind=kOutput, calls=%fused_computation.51 | convolution fusion | flops 549453824 | bytes 12582916 | tf_op jit(solution)/shard_map/akt,bkt->akb/dot_general | solution.py:16
  210.8 1.5 fusion.39
  212.3 3.9 %maximum_multiply_fusion = f32[128,2,32,256]{0,3,2,1:T(8,128)} fusion(f32[128,1,32,256]{0,3,2,1:T(8,128)S(1)} %fusion.39, f32[128,1,32,256]{0,3,2,1:T(8,128)S(1)} %fusion.40), kind=kLoop, calls=%fused_computation | loop fusion | flops 4194304 | bytes 16777216 | tf_op jit(solution)/shard_map/mul | solution.py:68
  216.1 10.2 %copy.13 = f32[128,2,32,256]{3,2,1,0:T(8,128)} copy(f32[128,2,32,256]{0,3,2,1:T(8,128)} %maximum_multiply_fusion) | data formatting | bytes 16777216 | tf_op jit(solution)/shard_map/mul | solution.py:68
  (9 shorter events, 0.1 us)
Async XLA Ops:
  6.5 186.7 %all-gather.2.cloned.1.call-start = ((), (), s32[]{:S(2)}) async-start(), calls=%async_computation.1 | async-start | bytes 6291456 | tf_op jit(solution)/shard_map/all_gather | solution.py:62
  8.9 6.2 %copy-start.2 = (s32[16,1024]{1,0:T(8,128)S(1)}, s32[16,1024]{1,0:T(8,128)}, u32[]{:S(2)}) copy-start(s32[16,1024]{1,0:T(8,128)} %param.3) | copy-start | bytes 196612
  10.3 16.0 %collective-permute-start = (bf16[16,15,1024]{2,1,0:T(8,128)(2,1)S(1)}, bf16[16,15,1024]{2,1,0:T(8,128)(2,1)S(1)}, u32[]{:S(2)}, u32[]{:S(2)}) collective-permute-start(bf16[16,15,1024]{2,1,0:T(8,128)(2,1)S(1)} %slice.143), channel_id=1, source_target_pairs={{0,1},{2,3},{4,5},{6,7},{8,9},{10,11},{12,13},{14,15},{16,17},{18,... | collective-permute-start | bytes 1474568 | tf_op jit(solution)/shard_map/ppermute | solution.py:12
  207.5 3.3 %copy-start = (bf16[256,32,128]{2,0,1:T(8,128)(2,1)S(1)}, bf16[256,32,128]{2,0,1:T(8,128)(2,1)}, u32[]{:S(2)}) copy-start(bf16[256,32,128]{2,0,1:T(8,128)(2,1)} %bitcast_negate_fusion) | copy-start | bytes 6291460
  207.5 3.3 %copy-start.1 = (bf16[256,32,1,128]{3,0,1,2:T(8,128)(2,1)S(1)}, bf16[256,32,1,128]{3,0,1,2:T(8,128)(2,1)}, u32[]{:S(2)}) copy-start(bf16[256,32,1,128]{3,0,1,2:T(8,128)(2,1)} %copy.16) | copy-start | bytes 6291460
Sparse Core Ops, SparseCore 0:
  135.0 58.1 all-gather.1
where the time goes:
time: 234 us; the launch traced here: 233 us
  waiting for transfers between devices  60.2 us (26%)
  local copies, waits for them, and re-layouts  54.1 us (23%)
  blocking collectives  53 us (23%)
  matrix products  29.7 us (13%)
  other arithmetic  17.9 us (8%)
  between operations  13.5 us (6%)
  starting transfers between devices  4.91 us (2%)
    all_gather x1, waiting for transfers between devices, shards(): segment = lax.all_gather(split_parts, 'tm', axis=3, tiled=True)  58.3 us
    all_to_all x1, blocking collectives, shards(): lax.all_to_all(packed, 'wide', split_axis=1, concat_axis=0, tiled=True)  53 us
    dot_general x1, matrix products, shards(): jnp.einsum('asl,lrc->acrs', filtered, dft_table, precision=lax.Precision....  24.9 us
    reshape x2, local copies, waits for them, and re-layouts, shards(): split_parts = arrived.reshape(all_inputs, local_channels, 2, spectra_dev)  11.5 us
    convert_element_type x1, local copies, waits for them, and re-layouts, shards(): spectra = jnp.einsum('asl,lrc->acrs', filtered, dft_table, precision=lax....  10.7 us
    mul x1, local copies, waits for them, and re-layouts, shards(): return summed * norm_factor  10.2 us
    neg x1, other arithmetic, shards(): -jnp.sin(angles)  9.21 us
    unnamed x9, local copies, waits for them, and re-layouts  9.12 us
  transfers between devices with their start and end apart: 2, of which 2 were waited for; matrix products, arithmetic and copies ran while one was open for 4% of the time, Pallas kernels for 0%

commit v1 on v0

v1 whole, which is shorter than its diff:
```python
import functools

import jax
import jax.numpy as jnp
import ml_dtypes
import numpy as np
from jax import lax
from jax.experimental import pallas as pl
from jax.experimental.pallas import tpu as pltpu
from jax.sharding import PartitionSpec as P

FIR_SCALE = 2.0 ** (-12)
MESH = pl.DeviceIdType.MESH
SUBLANES = 8
LANES = 128
VMEM_BYTES = 56 * 1024 * 1024


def dft_tables(length, widen):
    half = length // 2
    group = half // 2 // widen
    sample = np.arange(half)
    tables = []
    for parity in range(2):
        channel = 2 * np.arange(half // 2).reshape(widen, group) + parity
        angle = 2.0 * np.pi / length * (channel[:, :, None] * sample % length)
        table = np.stack([np.cos(angle), -np.sin(angle)], axis=1)
        table = table.reshape(widen * 2 * group, half) * (FIR_SCALE * length ** (-0.5))
        high = table.astype(ml_dtypes.bfloat16)
        low = (table - high.astype(np.float64)).astype(ml_dtypes.bfloat16)
        tables.append(np.concatenate([high, high, low], axis=1))
    return np.stack(tables)


def spectra_kernel(widen, volt_ref, halo_ref, taps_ref, table_ref, out_ref, folded, product, turned):
    inputs = volt_ref.shape[0]
    lags, length = taps_ref.shape
    frames = volt_ref.shape[1] // length
    half = length // 2
    chunks = half // LANES
    groups = inputs // SUBLANES
    group = half // 2 // widen
    columns = 256
    step = 8

    def frame(s, rows, lane):
        if s >= 0:
            return volt_ref[rows, pl.ds(s * length + lane, LANES)].astype(jnp.float32)
        at = (s + lags - 1) * length + lane
        return halo_ref[rows, pl.ds(at, LANES)].astype(jnp.float32)

    @pl.loop(0, groups * chunks)
    def fir(index):
        g = index // chunks
        c = index % chunks
        rows = pl.ds(pl.multiple_of(g * SUBLANES, SUBLANES), SUBLANES)
        for first in range(0, frames, step):
            sums = []
            for part in range(2):
                lane = pl.multiple_of(c * LANES, LANES) + part * half
                window = {s: frame(s, rows, lane) for s in range(first - lags + 1, first + step)}
                taps = [
                    taps_ref[pl.ds(p, 1), pl.ds(lane, LANES)].astype(jnp.float32)
                    for p in range(lags)
                ]
                totals = []
                for s in range(first, first + step):
                    total = taps[0] * window[s]
                    for p in range(1, lags):
                        total = total + taps[p] * window[s - p]
                    totals.append(total)
                sums.append(totals)
            for i in range(step):
                at = pl.ds(g * (SUBLANES * frames) + first + i, SUBLANES, stride=frames)
                folded[c, at, :] = sums[0][i] + sums[1][i]
                folded[chunks + c, at, :] = sums[0][i] - sums[1][i]

    pairs = columns // LANES
    blocks = inputs * frames // columns
    low_lanes = lax.broadcasted_iota(jnp.int32, (group, LANES), 1) < frames
    for parity in range(2):

        @pl.loop(0, blocks)
        def dft(block):
            rows = pl.ds(pl.multiple_of(block * columns, columns), columns)
            high, low = [], []
            for c in range(chunks):
                value = folded[parity * chunks + c, rows, :]
                top = value.astype(jnp.bfloat16)
                high.append(top)
                low.append((value - top.astype(jnp.float32)).astype(jnp.bfloat16))
            operand = jnp.concatenate(high + low + high, axis=1)
            product[...] = lax.dot_general(
                table_ref[parity], operand, (((1,), (1,)), ((), ())),
                preferred_element_type=jnp.float32,
            )

            @pl.loop(0, widen)
            def turn(d):
                at = pl.multiple_of(d * 2 * group, SUBLANES)
                for pair in range(pairs):
                    lanes = pl.ds(pair * LANES, LANES)
                    re = product[pl.ds(at, group), lanes]
                    im = product[pl.ds(at + group, group), lanes]
                    first = jnp.where(low_lanes, re, pltpu.roll(im, frames, 1))
                    second = jnp.where(low_lanes, pltpu.roll(re, frames, 1), im)
                    a = (block * pairs + pair) * 2
                    base = d * (group * inputs) + a
                    turned[pl.ds(base, group, stride=inputs), :] = first
                    turned[pl.ds(base + 1, group, stride=inputs), :] = second

        @pl.loop(0, widen)
        def cast(d):
            rows = pl.ds(pl.multiple_of(d * (group * inputs), group * inputs), group * inputs)
            out_ref[d, pl.ds(parity * group * inputs, group * inputs), :] = turned[rows, :].astype(
                jnp.bfloat16
            )


def spectra_of(voltages, halo, taps, widen):
    inputs = voltages.shape[0]
    length = taps.shape[1]
    frames = voltages.shape[1] // length
    half = length // 2
    table = jnp.asarray(dft_tables(length, widen))
    rows = half // widen * inputs
    return pl.pallas_call(
        functools.partial(spectra_kernel, widen),
        out_shape=jax.ShapeDtypeStruct((widen, rows, 2 * frames), jnp.bfloat16),
        in_specs=[pl.BlockSpec(memory_space=pltpu.VMEM)] * 4,
        out_specs=pl.BlockSpec(memory_space=pltpu.VMEM),
        scratch_shapes=[
            pltpu.VMEM((2 * half // LANES, inputs * frames, LANES), jnp.float32),
            pltpu.VMEM((half, 256), jnp.float32),
            pltpu.VMEM((half // 2 * inputs, LANES), jnp.float32),
        ],
        compiler_params=pltpu.CompilerParams(vmem_limit_bytes=VMEM_BYTES),
        cost_estimate=pl.CostEstimate(
            flops=6 * half * length * inputs * frames, bytes_accessed=12 << 20, transcendentals=0
        ),
        name="spectra",
    )(voltages, halo, taps, table)


def flipped(index, bits):
    bit = 1
    while bit <= bits:
        if bits & bit:
            index = index + bit - 2 * bit * ((index // bit) % 2)
        bit *= 2
    return index


def send_order(widen):
    far = [i for i in range(widen // 2, widen)]
    near = [i for i in range(2, widen // 2)]
    order = [1]
    while far or near:
        order += far[:2] + near[:1]
        far, near = far[2:], near[1:]
    return order


def exchange_kernel(widen, ranks, spec_ref, out_ref, own_sem, send_wide, recv_wide, send_tm, recv_tm):
    w = lax.axis_index("wide")
    t = lax.axis_index("tm")
    order = send_order(widen)

    barrier = pltpu.get_barrier_semaphore()
    for i in order:
        pl.semaphore_signal(barrier, inc=1, device_id=(flipped(w, i), t), device_id_type=MESH)
    for r in range(1, ranks):
        pl.semaphore_signal(
            barrier, inc=1, device_id=(w, lax.rem(t + r, ranks)), device_id_type=MESH
        )
    pl.semaphore_wait(barrier, len(order) + ranks - 1)

    def onward(src_ref, i, r):
        return pltpu.make_async_remote_copy(
            src_ref=src_ref,
            dst_ref=out_ref.at[t, flipped(w, i)],
            send_sem=send_tm.at[i, r - 1],
            recv_sem=recv_tm.at[i, r - 1],
            device_id=(w, lax.rem(t + r, ranks)),
            device_id_type=MESH,
        )

    own = pltpu.make_async_copy(spec_ref.at[w], out_ref.at[t, w], own_sem)
    own.start()
    copies = []
    for r in range(1, ranks):
        copy = onward(spec_ref.at[w], 0, r)
        copy.start()
        copies.append(copy)
    across = []
    for i in order:
        partner = flipped(w, i)
        copy = pltpu.make_async_remote_copy(
            src_ref=spec_ref.at[partner],
            dst_ref=out_ref.at[t, w],
            send_sem=send_wide.at[i],
            recv_sem=recv_wide.at[i],
            device_id=(partner, t),
            device_id_type=MESH,
        )
        copy.start()
        across.append(copy)
    for i, copy in zip(order, across):
        copy.wait_recv()
        for r in range(1, ranks):
            passed = onward(out_ref.at[t, flipped(w, i)], i, r)
            passed.start()
            copies.append(passed)
    own.wait()
    for copy in across:
        copy.wait_send()
    for copy in copies:
        copy.wait()


def exchanged(spectra, widen, ranks):
    return pl.pallas_call(
        functools.partial(exchange_kernel, widen, ranks),
        out_shape=jax.ShapeDtypeStruct((ranks,) + spectra.shape, spectra.dtype),
        in_specs=[pl.BlockSpec(memory_space=pl.ANY)],
        out_specs=pl.BlockSpec(memory_space=pl.ANY),
        scratch_shapes=[
            pltpu.SemaphoreType.DMA(()),
            pltpu.SemaphoreType.DMA((widen,)),
            pltpu.SemaphoreType.DMA((widen,)),
            pltpu.SemaphoreType.DMA((widen, ranks - 1)),
            pltpu.SemaphoreType.DMA((widen, ranks - 1)),
        ],
        compiler_params=pltpu.CompilerParams(collective_id=0, has_side_effects=True),
        name="exchange",
    )(spectra)


def shards(voltages, taps):
    local_inputs = voltages.shape[0]
    lags, length = taps.shape
    frames = voltages.shape[1] // length
    widen = lax.axis_size("wide")
    ranks = lax.axis_size("tm")
    channels = length // 2 // widen
    norm = 1.0 / (frames * ranks)

    tail = voltages[:, (frames - lags + 1) * length :].astype(jnp.bfloat16)
    halo = lax.ppermute(tail, "tm", [(i, i + 1) for i in range(ranks - 1)])
    spectra = spectra_of(voltages, halo, taps, widen)
    full = exchanged(spectra, widen, ranks)
    return gram_rows(full, local_inputs, channels, norm)


def gram_rows(full, inputs, channels, norm):
    ranks, widen, rows, width = full.shape
    total = widen * inputs
    own = total // ranks
    step = SUBLANES
    group = channels // 2
    first = (lax.axis_index("tm") * (own // inputs)).astype(jnp.int32).reshape(1)
    pairs = step // 2
    split = full.reshape(ranks, widen, 2, group * inputs, width)

    def kernel(first_ref, even_ref, odd_ref, out_ref):
        own_from = first_ref[0]
        lane = lax.broadcasted_iota(jnp.int32, (own, width), 1)
        sign = jnp.where(lane < width // 2, norm, -norm)
        for k in range(step):
            ref = (even_ref, odd_ref)[k % 2]
            at = pl.ds(k // 2 * inputs, inputs)
            whole = jnp.concatenate(
                [ref[t, :, 0, at, :].reshape(total, width) for t in range(ranks)], axis=1
            )
            mine = [
                ref[t, pl.ds(own_from, own // inputs), 0, at, :].reshape(own, width)
                for t in range(ranks)
            ]
            rotated = [
                (pltpu.roll(x.astype(jnp.float32), width // 2, 1) * sign).astype(jnp.bfloat16)
                for x in mine
            ]
            scaled = [(x.astype(jnp.float32) * norm).astype(jnp.bfloat16) for x in mine]
            left = jnp.concatenate(
                [jnp.concatenate(scaled, axis=1), jnp.concatenate(rotated, axis=1)], axis=0
            )
            gram = lax.dot_general(
                left, whole, (((1,), (1,)), ((), ())), preferred_element_type=jnp.float32
            )
            out_ref[:, 0, k, :] = gram[:own]
            out_ref[:, 1, k, :] = gram[own:]

    block = (ranks, widen, 1, pairs * inputs, width)
    return pl.pallas_call(
        kernel,
        grid=(channels // step,),
        out_shape=jax.ShapeDtypeStruct((own, 2, channels, total), jnp.float32),
        in_specs=[
            pl.BlockSpec(memory_space=pltpu.SMEM),
            pl.BlockSpec(block, lambda i: (0, 0, 0, i, 0)),
            pl.BlockSpec(block, lambda i: (0, 0, 1, i, 0)),
        ],
        out_specs=pl.BlockSpec((own, 2, step, total), lambda i: (0, 0, i, 0)),
        compiler_params=pltpu.CompilerParams(vmem_limit_bytes=VMEM_BYTES),
        name="gram",
    )(first, split, split)


def solution(mesh):
    placed = (P("wide", "tm"), P())
    return jax.shard_map(
        shards, mesh=mesh, in_specs=placed, out_specs=P("tm", None, "wide", None), check_vma=False
    )
```

time: 234 us -> 129 us (0.55)
  Pallas kernels: 0 us -> 111 us
  local copies, waits for them, and re-layouts: 54.1 us -> 0.78 us
  blocking collectives: 53 us -> 0 us
  waiting for transfers between devices: 60.2 us -> 10.4 us
  matrix products: 29.7 us -> 0 us
  other arithmetic: 17.9 us -> 1.25 us
  between operations: 13.5 us -> 0.03 us
    pallas_call x0 -> x3, Pallas kernels: none -> 111 us  [the longest x1 75.4 us: exchanged(): pl.pallas_call(functools.partial(exchange_kernel, widen, ranks), out_shap...]
    all_gather x1 -> x0, waiting for transfers between devices: 58.3 us -> none  [shards(): segment = lax.all_gather(split_parts, 'tm', axis=3, tiled=True)]
    all_to_all x1 -> x0, blocking collectives: 53 us -> none  [shards(): lax.all_to_all(packed, 'wide', split_axis=1, concat_axis=0, tiled=True)]
    dot_general x3 -> x0, matrix products: 29.7 us -> none  [the longest x1 24.9 us: shards(): jnp.einsum('asl,lrc->acrs', filtered, dft_table, precision=lax.Precision....]
    reshape x4 -> x0, local copies, waits for them, and re-layouts: 19.1 us -> none  [the longest x2 11.5 us: shards(): split_parts = arrived.reshape(all_inputs, local_channels, 2, spectra_dev)]
    neg x2 -> x0, other arithmetic: 10.8 us -> none  [the longest x1 9.21 us: shards(): -jnp.sin(angles)]
    convert_element_type x1 -> x0, local copies, waits for them, and re-layouts: 10.7 us -> none  [shards(): spectra = jnp.einsum('asl,lrc->acrs', filtered, dft_table, precision=lax....]
    mul x1 -> x0, local copies, waits for them, and re-layouts: 10.2 us -> none  [shards(): return summed * norm_factor]
  transfers between devices with their start and end apart: 2 -> 1, of which waited for: 2 -> 1; matrix products, arithmetic and copies ran while one was open for 4% -> 0% of each run, Pallas kernels for 0% -> 0%
where the time goes in v1:
time: 129 us
  Pallas kernels  111 us (86%)
  waiting for transfers between devices  10.4 us (8%)
  starting transfers between devices  4.9 us (4%)
    pallas_call x1, Pallas kernels, exchanged(): pl.pallas_call(functools.partial(exchange_kernel, widen, ranks), out_shap...  75.4 us
    pallas_call x1, Pallas kernels, spectra_of(): pl.pallas_call(functools.partial(spectra_kernel, widen), out_shape=jax.Sh...  28.1 us
    ppermute x1, waiting for transfers between devices, shards(): halo = lax.ppermute(tail, 'tm', [(i, i + 1) for i in range(ranks - 1)])  10.4 us
    pallas_call x1, Pallas kernels, gram_rows(): pl.pallas_call(kernel, grid=(channels // step,), out_shape=jax.ShapeDtype...  7.7 us
    ppermute x1, starting transfers between devices, shards(): halo = lax.ppermute(tail, 'tm', [(i, i + 1) for i in range(ranks - 1)])  4.9 us
  transfers between devices with their start and end apart: 1, of which 1 were waited for; matrix products, arithmetic and copies ran while one was open for 0% of the time, Pallas kernels for 0%

profile of v1, /device:TPU:0, one launch (start us, length us, event | category | flops | bytes accessed | tf_op | source)
XLA Modules:
  0.0 128.5 jit_solution(17360050658216951675)
XLA Ops:
  0.0 1.3 slice_convert_fusion
  1.3 4.9 %collective-permute-start = (bf16[16,15360]{1,0:T(8,128)(2,1)S(1)}, bf16[16,15360]{1,0:T(8,128)(2,1)S(1)}, u32[]{:S(2)}, u32[]{:S(2)}) collective-permute-start(bf16[16,15360]{1,0:T(8,128)(2,1)S(1)} %slice_convert_fusion), channel_id=1, source_target_pairs={{0,1},{2,3},{4,5},{6,7},{8,9},{10,11},{12,13},{14,15},{16,17},{18,... | collective-permute-start | bytes 1474568 | tf_op jit(solution)/shard_map/ppermute | solution.py:249
  6.2 10.4 %collective-permute-done.halo_ref = bf16[16,15360]{1,0:T(8,128)(2,1)S(1)} collective-permute-done((bf16[16,15360]{1,0:T(8,128)(2,1)S(1)}, bf16[16,15360]{1,0:T(8,128)(2,1)S(1)}, u32[]{:S(2)}, u32[]{:S(2)}) %collective-permute-start) | collective-permute-done | bytes 491552 | tf_op jit(solution)/shard_map/ppermute | solution.py:249
  16.6 0.0 copy-start
  16.6 0.8 copy-done
  17.4 28.1 %spectra.1.spec_ref = bf16[16,512,128]{2,1,0:T(8,128)(2,1)} custom-call(s32[16,65536]{1,0:T(8,128)} %volt_ref.1, bf16[16,15360]{1,0:T(8,128)(2,1)} %copy-done, s32[16,1024]{1,0:T(8,128)} %taps_ref.1, bf16[2,512,1536]{2,1,0:T(8,128)(2,1)} %constant.8.clone.table_ref), custom_call_target="tpu_custom_call" | custom-call | flops 3221225472 | bytes 12582912 | tf_op jit(solution)/shard_map/spectra/pallas_call | solution.py:127
  45.4 75.4 %exchange.1 = bf16[2,16,512,128]{3,2,1,0:T(8,128)(2,1)} custom-call(bf16[16,512,128]{2,1,0:T(8,128)(2,1)} %spectra.1.spec_ref), custom_call_target="tpu_custom_call" | custom-call | tf_op jit(solution)/shard_map/exchange/pallas_call | solution.py:222
  120.8 7.7 %gram.1 = f32[128,2,32,256]{3,2,1,0:T(8,128)} custom-call(s32[1]{0:T(128)} %bitcast.first_ref, bf16[2,16,2,256,128]{4,3,2,1,0:T(8,128)(2,1)} %bitcast.2, bf16[2,16,2,256,128]{4,3,2,1,0:T(8,128)(2,1)} %bitcast.3), custom_call_target="tpu_custom_call" | custom-call | tf_op jit(solution)/shard_map/gram/pallas_call | solution.py:294
Async XLA Ops:
  1.3 15.3 %collective-permute-start = (bf16[16,15360]{1,0:T(8,128)(2,1)S(1)}, bf16[16,15360]{1,0:T(8,128)(2,1)S(1)}, u32[]{:S(2)}, u32[]{:S(2)}) collective-permute-start(bf16[16,15360]{1,0:T(8,128)(2,1)S(1)} %slice_convert_fusion), channel_id=1, source_target_pairs={{0,1},{2,3},{4,5},{6,7},{8,9},{10,11},{12,13},{14,15},{16,17},{18,... | collective-permute-start | bytes 1474568 | tf_op jit(solution)/shard_map/ppermute | solution.py:249
  16.6 0.8 copy-start

commit v2 on v1

v2 whole, which is shorter than its diff:
```python
import functools

import jax
import jax.numpy as jnp
import ml_dtypes
import numpy as np
from jax import lax
from jax.experimental import pallas as pl
from jax.experimental.pallas import tpu as pltpu
from jax.sharding import PartitionSpec as P

FIR_SCALE = 2.0 ** (-12)
MESH = pl.DeviceIdType.MESH
SUBLANES = 8
LANES = 128
STEP = 16
COLUMNS = 256
WINDOW = 8
VMEM_BYTES = 56 * 1024 * 1024


def dft_tables(length, widen):
    half = length // 2
    group = half // 2 // widen
    sample = np.arange(half)
    tables = []
    for parity in range(2):
        channel = 2 * np.arange(half // 2).reshape(widen, group) + parity
        angle = 2.0 * np.pi / length * (channel[:, :, None] * sample % length)
        table = np.stack([np.cos(angle), -np.sin(angle)], axis=1)
        table = table.reshape(widen * 2 * group, half) * (FIR_SCALE * length ** (-0.5))
        high = table.astype(ml_dtypes.bfloat16)
        low = (table - high.astype(np.float64)).astype(ml_dtypes.bfloat16)
        tables.append(np.concatenate([high, high, low], axis=1))
    return np.stack(tables)


def flipped(index, bits):
    bit = 1
    while bit <= bits:
        if bits & bit:
            index = index + bit - 2 * bit * ((index // bit) % 2)
        bit *= 2
    return index


def send_order(widen):
    far = [i for i in range(widen // 2, widen)]
    near = [i for i in range(2, widen // 2)]
    order = [1]
    while far or near:
        order += far[:2] + near[:1]
        far, near = far[2:], near[1:]
    return order


def spectra_kernel(
    widen, ranks, volt_ref, taps_ref, table_hbm, out_ref,
    tail, halo, before, table_ref, folded, turned, spec,
    table_sem, own_sem, halo_sems, send_wide, recv_wide, send_tm, recv_tm,
):
    w = lax.axis_index("wide")
    t = lax.axis_index("tm")
    inputs = volt_ref.shape[0]
    lags, length = taps_ref.shape
    frames = volt_ref.shape[1] // length
    half = length // 2
    chunks = half // LANES
    groups = inputs // SUBLANES
    group = half // 2 // widen
    order = send_order(widen)

    barrier = pltpu.get_barrier_semaphore()
    for i in order:
        pl.semaphore_signal(barrier, inc=1, device_id=(flipped(w, i), t), device_id_type=MESH)
    for r in range(1, ranks):
        pl.semaphore_signal(
            barrier, inc=1, device_id=(w, lax.rem(t + r, ranks)), device_id_type=MESH
        )
    load_table = pltpu.make_async_copy(table_hbm, table_ref, table_sem)
    load_table.start()
    from_frame = (frames - lags + 1) * length
    for p in range(lags - 1):
        at = pl.ds(p * length, length)
        tail[:, at] = volt_ref[:, pl.ds(from_frame + p * length, length)].astype(jnp.bfloat16)
    pl.semaphore_wait(barrier, len(order) + ranks - 1)

    halo_copy = pltpu.make_async_remote_copy(
        src_ref=tail, dst_ref=halo, send_sem=halo_sems.at[0], recv_sem=halo_sems.at[1],
        device_id=(w, lax.rem(t + 1, ranks)), device_id_type=MESH,
    )

    @pl.when(t < ranks - 1)
    def send_halo():
        halo_copy.start()

    def fir(index, first, frame):
        g = index // chunks
        c = index % chunks
        rows = pl.ds(pl.multiple_of(g * SUBLANES, SUBLANES), SUBLANES)
        sums = []
        for part in range(2):
            lane = pl.multiple_of(c * LANES, LANES) + part * half
            window = jnp.stack([frame(i - (lags - 1), rows, lane) for i in range(STEP + lags - 1)])
            total = None
            for p in range(lags):
                tap = taps_ref[pl.ds(p, 1), pl.ds(lane, LANES)].astype(jnp.float32)
                term = tap * window[lags - 1 - p : lags - 1 - p + STEP]
                total = term if total is None else total + term
            sums.append(total)
        for number, value in enumerate((sums[0] + sums[1], sums[0] - sums[1])):
            for i in range(STEP):
                at = pl.ds(g * (SUBLANES * frames) + first + i, SUBLANES, stride=frames)
                folded[number * chunks + c, at, :] = value[i]

    later = frames // STEP - 1

    @pl.loop(0, groups * chunks * later)
    def fir_later(index):
        first = (1 + index % later) * STEP

        def frame(s, rows, lane):
            return volt_ref[rows, pl.ds((first + s) * length + lane, LANES)].astype(jnp.float32)

        fir(index // later, first, frame)

    @pl.when(t == 0)
    def no_halo():
        before[...] = jnp.zeros_like(before)

    @pl.when(t > 0)
    def wait_halo():
        halo_copy.wait_recv()
        for p in range(lags - 1):
            at = pl.ds(p * length, length)
            before[:, at] = halo[:, at].astype(jnp.float32)

    @pl.loop(0, groups * chunks)
    def fir_first(index):
        def frame(s, rows, lane):
            if s < 0:
                at = pl.ds((s + lags - 1) * length + lane, LANES)
                return before[rows, at]
            return volt_ref[rows, pl.ds(s * length + lane, LANES)].astype(jnp.float32)

        fir(index, 0, frame)

    load_table.wait()
    pairs = COLUMNS // LANES
    blocks = inputs * frames // COLUMNS
    low_lanes = lax.broadcasted_iota(jnp.int32, (widen * group, LANES), 1) < frames

    def dft(parity, block):
        rows = pl.ds(pl.multiple_of(block * COLUMNS, COLUMNS), COLUMNS)
        high, low = [], []
        for c in range(chunks):
            value = folded[parity * chunks + c, rows, :]
            top = value.astype(jnp.bfloat16)
            high.append(top)
            low.append((value - top.astype(jnp.float32)).astype(jnp.bfloat16))
        operand = jnp.concatenate(high + low + high, axis=1)
        product = lax.dot_general(
            table_ref[parity], operand, (((1,), (1,)), ((), ())),
            preferred_element_type=jnp.float32,
        )
        for pair in range(pairs):
            part = product[:, pair * LANES : (pair + 1) * LANES]
            part = part.reshape(widen, 2, group, LANES)
            re = part[:, 0].reshape(widen * group, LANES)
            im = part[:, 1].reshape(widen * group, LANES)
            a = (block * pairs + pair) * 2
            turned[pl.ds(a, widen * group, stride=inputs), :] = jnp.where(
                low_lanes, re, pltpu.roll(im, frames, 1)
            )
            turned[pl.ds(a + 1, widen * group, stride=inputs), :] = jnp.where(
                low_lanes, pltpu.roll(re, frames, 1), im
            )

    def cast(parity):
        @pl.loop(0, widen)
        def one(d):
            rows = pl.ds(pl.multiple_of(d * (group * inputs), group * inputs), group * inputs)
            spec[d, parity] = turned[rows, :].astype(jnp.bfloat16)

    onward_copies, own_copies = [], []

    def pass_on(src_ref, parity, i):
        for r in range(1, ranks):
            copy = pltpu.make_async_remote_copy(
                src_ref=src_ref,
                dst_ref=out_ref.at[t, flipped(w, i), parity],
                send_sem=send_tm.at[parity, i, r - 1],
                recv_sem=recv_tm.at[parity, i, r - 1],
                device_id=(w, lax.rem(t + r, ranks)),
                device_id_type=MESH,
            )
            copy.start()
            onward_copies.append(copy)

    def own(parity):
        copy = pltpu.make_async_copy(
            spec.at[w, parity], out_ref.at[t, w, parity], own_sem.at[parity]
        )
        copy.start()
        own_copies.append(copy)
        pass_on(spec.at[w, parity], parity, 0)

    def across(parity, i):
        return pltpu.make_async_remote_copy(
            src_ref=spec.at[flipped(w, i), parity],
            dst_ref=out_ref.at[t, w, parity],
            send_sem=send_wide.at[parity, i],
            recv_sem=recv_wide.at[parity, i],
            device_id=(flipped(w, i), t),
            device_id_type=MESH,
        )

    sequence = [(parity, i) for parity in range(2) for i in order]
    started = []

    def start_next(limit):
        if len(started) < limit:
            copy = across(*sequence[len(started)])
            copy.start()
            started.append(copy)

    def handle(number, limit):
        parity, i = sequence[number]
        started[number].wait_recv()
        pass_on(out_ref.at[t, flipped(w, i), parity], parity, i)
        start_next(limit)

    @pl.loop(0, blocks)
    def dft_even(block):
        dft(0, block)

    cast(0)
    for _ in range(WINDOW):
        start_next(len(order))
    own(0)
    handled = 0
    for block in range(blocks):
        dft(1, block)
        handle(handled, len(order))
        handled += 1
    cast(1)
    own(1)
    while len(started) < handled + WINDOW:
        start_next(len(sequence))
    while handled < len(sequence):
        handle(handled, len(sequence))
        handled += 1

    for copy in own_copies:
        copy.wait()
    for copy in started:
        copy.wait_send()
    for copy in onward_copies:
        copy.wait()

    @pl.when(t < ranks - 1)
    def halo_sent():
        halo_copy.wait_send()


def exchanged_spectra(voltages, taps, widen, ranks):
    inputs = voltages.shape[0]
    lags, length = taps.shape
    frames = voltages.shape[1] // length
    half = length // 2
    table = jnp.asarray(dft_tables(length, widen))
    block = (2, half // 2 // widen * inputs, 2 * frames)
    halo_shape = (inputs, (lags - 1) * length)
    return pl.pallas_call(
        functools.partial(spectra_kernel, widen, ranks),
        out_shape=jax.ShapeDtypeStruct((ranks, widen) + block, jnp.bfloat16),
        in_specs=[
            pl.BlockSpec(memory_space=pltpu.VMEM),
            pl.BlockSpec(memory_space=pltpu.VMEM),
            pl.BlockSpec(memory_space=pl.ANY),
        ],
        out_specs=pl.BlockSpec(memory_space=pl.ANY),
        scratch_shapes=[
            pltpu.VMEM(halo_shape, jnp.bfloat16),
            pltpu.VMEM(halo_shape, jnp.bfloat16),
            pltpu.VMEM(halo_shape, jnp.float32),
            pltpu.VMEM(table.shape, jnp.bfloat16),
            pltpu.VMEM((2 * half // LANES, inputs * frames, LANES), jnp.float32),
            pltpu.VMEM((half // 2 * inputs, LANES), jnp.float32),
            pltpu.VMEM((widen,) + block, jnp.bfloat16),
            pltpu.SemaphoreType.DMA(()),
            pltpu.SemaphoreType.DMA((2,)),
            pltpu.SemaphoreType.DMA((2,)),
            pltpu.SemaphoreType.DMA((2, widen)),
            pltpu.SemaphoreType.DMA((2, widen)),
            pltpu.SemaphoreType.DMA((2, widen, ranks - 1)),
            pltpu.SemaphoreType.DMA((2, widen, ranks - 1)),
        ],
        compiler_params=pltpu.CompilerParams(
            collective_id=0, has_side_effects=True, vmem_limit_bytes=VMEM_BYTES
        ),
        name="spectra_exchange",
    )(voltages, taps, table)


def shards(voltages, taps):
    local_inputs = voltages.shape[0]
    lags, length = taps.shape
    frames = voltages.shape[1] // length
    widen = lax.axis_size("wide")
    ranks = lax.axis_size("tm")
    channels = length // 2 // widen
    norm = 1.0 / (frames * ranks)

    full = exchanged_spectra(voltages, taps, widen, ranks)
    return gram_rows(full, local_inputs, channels, norm)


def gram_rows(full, inputs, channels, norm):
    ranks, widen, _, _, width = full.shape
    total = widen * inputs
    own = total // ranks
    step = SUBLANES
    first = (lax.axis_index("tm") * (own // inputs)).astype(jnp.int32).reshape(1)
    pairs = step // 2

    def kernel(first_ref, even_ref, odd_ref, out_ref):
        own_from = first_ref[0]
        lane = lax.broadcasted_iota(jnp.int32, (own, width), 1)
        sign = jnp.where(lane < width // 2, norm, -norm)
        for k in range(step):
            ref = (even_ref, odd_ref)[k % 2]
            at = pl.ds(k // 2 * inputs, inputs)
            whole = jnp.concatenate(
                [ref[t, :, 0, at, :].reshape(total, width) for t in range(ranks)], axis=1
            )
            mine = [
                ref[t, pl.ds(own_from, own // inputs), 0, at, :].reshape(own, width)
                for t in range(ranks)
            ]
            rotated = [
                (pltpu.roll(x.astype(jnp.float32), width // 2, 1) * sign).astype(jnp.bfloat16)
                for x in mine
            ]
            scaled = [(x.astype(jnp.float32) * norm).astype(jnp.bfloat16) for x in mine]
            left = jnp.concatenate(
                [jnp.concatenate(scaled, axis=1), jnp.concatenate(rotated, axis=1)], axis=0
            )
            gram = lax.dot_general(
                left, whole, (((1,), (1,)), ((), ())), preferred_element_type=jnp.float32
            )
            out_ref[:, 0, k, :] = gram[:own]
            out_ref[:, 1, k, :] = gram[own:]

    block = (ranks, widen, 1, pairs * inputs, width)
    return pl.pallas_call(
        kernel,
        grid=(channels // step,),
        out_shape=jax.ShapeDtypeStruct((own, 2, channels, total), jnp.float32),
        in_specs=[
            pl.BlockSpec(memory_space=pltpu.SMEM),
            pl.BlockSpec(block, lambda i: (0, 0, 0, i, 0)),
            pl.BlockSpec(block, lambda i: (0, 0, 1, i, 0)),
        ],
        out_specs=pl.BlockSpec((own, 2, step, total), lambda i: (0, 0, i, 0)),
        compiler_params=pltpu.CompilerParams(vmem_limit_bytes=VMEM_BYTES),
        name="gram",
    )(first, full, full)


def solution(mesh):
    placed = (P("wide", "tm"), P())
    return jax.shard_map(
        shards, mesh=mesh, in_specs=placed, out_specs=P("tm", None, "wide", None), check_vma=False
    )
```

time: 129 us -> 94.3 us (0.73)
  the two profiles are of different devices: /device:TPU:0 before, /device:TPU:17 now
where the time goes in v2:
time: 94.3 us; the launch traced here: 94.1 us
  Pallas kernels  94.1 us (100%)
    pallas_call x1, Pallas kernels, exchanged_spectra(): pl.pallas_call(functools.partial(spectra_kernel, widen, ranks), out_shape...  86.4 us
    pallas_call x1, Pallas kernels, gram_rows(): pl.pallas_call(kernel, grid=(channels // step,), out_shape=jax.ShapeDtype...  7.7 us

profile of v2, /device:TPU:17, one launch (start us, length us, event | category | flops | bytes accessed | tf_op | source)
XLA Modules:
  0.0 94.1 jit_solution(5974687706229128595)
XLA Ops:
  0.0 86.4 %spectra_exchange.1.even_ref.odd_ref = bf16[2,16,2,256,128]{4,3,2,1,0:T(8,128)(2,1)} custom-call(s32[16,65536]{1,0:T(8,128)} %volt_ref.1, s32[16,1024]{1,0:T(8,128)} %taps_ref.1, bf16[2,512,1536]{2,1,0:T(8,128)(2,1)} %constant.8.clone.table_hbm), custom_call_target="tpu_custom_call" | custom-call | tf_op jit(solution)/shard_map/spectra_exchange/pallas_call | solution.py:274
  86.4 7.7 %gram.1 = f32[128,2,32,256]{3,2,1,0:T(8,128)} custom-call(s32[1]{0:T(128)} %bitcast.first_ref, bf16[2,16,2,256,128]{4,3,2,1,0:T(8,128)(2,1)} %spectra_exchange.1.even_ref.odd_ref, bf16[2,16,2,256,128]{4,3,2,1,0:T(8,128)(2,1)} %spectra_exchange.1.even_ref.odd_ref), custom_call_target="tpu_custom_call" | custom-call | tf_op jit(solution)/shard_map/gram/pallas_call | solution.py:356

commit v3 on v2

--- a/solution.py
+++ b/solution.py
@@ -56,7 +56,7 @@
 
 def spectra_kernel(
     widen, ranks, volt_ref, taps_ref, table_hbm, out_ref,
-    tail, halo, before, table_ref, folded, turned, spec,
+    tail, halo, before, table_ref, folded, product, turned, spec,
     table_sem, own_sem, halo_sems, send_wide, recv_wide, send_tm, recv_tm,
 ):
     w = lax.axis_index("wide")
@@ -93,6 +93,8 @@
     @pl.when(t < ranks - 1)
     def send_halo():
         halo_copy.start()
+
+    span = frames // 2
 
     def fir(index, first, frame):
         g = index // chunks
@@ -110,77 +112,86 @@
             sums.append(total)
         for number, value in enumerate((sums[0] + sums[1], sums[0] - sums[1])):
             for i in range(STEP):
-                at = pl.ds(g * (SUBLANES * frames) + first + i, SUBLANES, stride=frames)
+                at = pl.ds(g * (SUBLANES * span) + first % span + i, SUBLANES, stride=span)
                 folded[number * chunks + c, at, :] = value[i]
 
-    later = frames // STEP - 1
-
-    @pl.loop(0, groups * chunks * later)
-    def fir_later(index):
-        first = (1 + index % later) * STEP
-
-        def frame(s, rows, lane):
-            return volt_ref[rows, pl.ds((first + s) * length + lane, LANES)].astype(jnp.float32)
-
-        fir(index // later, first, frame)
-
-    @pl.when(t == 0)
-    def no_halo():
-        before[...] = jnp.zeros_like(before)
-
-    @pl.when(t > 0)
-    def wait_halo():
-        halo_copy.wait_recv()
-        for p in range(lags - 1):
-            at = pl.ds(p * length, length)
-            before[:, at] = halo[:, at].astype(jnp.float32)
-
-    @pl.loop(0, groups * chunks)
-    def fir_first(index):
-        def frame(s, rows, lane):
-            if s < 0:
-                at = pl.ds((s + lags - 1) * length + lane, LANES)
-                return before[rows, at]
-            return volt_ref[rows, pl.ds(s * length + lane, LANES)].astype(jnp.float32)
-
-        fir(index, 0, frame)
-
-    load_table.wait()
-    pairs = COLUMNS // LANES
-    blocks = inputs * frames // COLUMNS
-    low_lanes = lax.broadcasted_iota(jnp.int32, (widen * group, LANES), 1) < frames
-
-    def dft(parity, block):
+    def fir_later(first):
+        @pl.loop(0, groups * chunks)
+        def run(index):
+            def frame(s, rows, lane):
+                at = pl.ds((first + s) * length + lane, LANES)
+                return volt_ref[rows, at].astype(jnp.float32)
+
+            fir(index, first, frame)
+
+    def fir_first():
+        @pl.when(t == 0)
+        def no_halo():
+            before[...] = jnp.zeros_like(before)
+
+        @pl.when(t > 0)
+        def wait_halo():
+            halo_copy.wait_recv()
+            for p in range(lags - 1):
+                at = pl.ds(p * length, length)
+                before[:, at] = halo[:, at].astype(jnp.float32)
+
+        @pl.loop(0, groups * chunks)
+        def run(index):
+            def frame(s, rows, lane):
+                if s < 0:
+                    return before[rows, pl.ds((s + lags - 1) * length + lane, LANES)]
+                return volt_ref[rows, pl.ds(s * length + lane, LANES)].astype(jnp.float32)
+
+            fir(index, 0, frame)
+
+    tiles = COLUMNS // LANES
+    blocks = inputs * span // COLUMNS
+    lane_at = lax.broadcasted_iota(jnp.int32, (widen * group, LANES), 1)
+    lower = lane_at < 2 * span
+    even = (lane_at // span) % 2 == 0
+
+    def dft(block):
         rows = pl.ds(pl.multiple_of(block * COLUMNS, COLUMNS), COLUMNS)
-        high, low = [], []
-        for c in range(chunks):
-            value = folded[parity * chunks + c, rows, :]
-            top = value.astype(jnp.bfloat16)
-            high.append(top)
-            low.append((value - top.astype(jnp.float32)).astype(jnp.bfloat16))
-        operand = jnp.concatenate(high + low + high, axis=1)
-        product = lax.dot_general(
-            table_ref[parity], operand, (((1,), (1,)), ((), ())),
-            preferred_element_type=jnp.float32,
-        )
-        for pair in range(pairs):
-            part = product[:, pair * LANES : (pair + 1) * LANES]
-            part = part.reshape(widen, 2, group, LANES)
-            re = part[:, 0].reshape(widen * group, LANES)
-            im = part[:, 1].reshape(widen * group, LANES)
-            a = (block * pairs + pair) * 2
-            turned[pl.ds(a, widen * group, stride=inputs), :] = jnp.where(
-                low_lanes, re, pltpu.roll(im, frames, 1)
+        for parity in range(2):
+            high, low = [], []
+            for c in range(chunks):
+                value = folded[parity * chunks + c, rows, :]
+                top = value.astype(jnp.bfloat16)
+                high.append(top)
+                low.append((value - top.astype(jnp.float32)).astype(jnp.bfloat16))
+            operand = jnp.concatenate(high + low + high, axis=1)
+            product[parity] = lax.dot_general(
+                table_ref[parity], operand, (((1,), (1,)), ((), ())),
+                preferred_element_type=jnp.float32,
             )
-            turned[pl.ds(a + 1, widen * group, stride=inputs), :] = jnp.where(
-                low_lanes, pltpu.roll(re, frames, 1), im
-            )
-
-    def cast(parity):
+        for tile in range(tiles):
+            parts = []
+            for parity in range(2):
+                part = product[parity, :, tile * LANES : (tile + 1) * LANES]
+                part = part.reshape(widen, 2, group, LANES)
+                parts.append(part[:, 0].reshape(widen * group, LANES))
+                parts.append(part[:, 1].reshape(widen * group, LANES))
+            x0, x1, x2, x3 = parts
+            y0 = jnp.where(lower, x0, pltpu.roll(x2, 2 * span, 1))
+            y2 = jnp.where(lower, pltpu.roll(x0, 2 * span, 1), x2)
+            y1 = jnp.where(lower, x1, pltpu.roll(x3, 2 * span, 1))
+            y3 = jnp.where(lower, pltpu.roll(x1, 2 * span, 1), x3)
+            swapped = [
+                jnp.where(even, y0, pltpu.roll(y1, span, 1)),
+                jnp.where(even, pltpu.roll(y0, 3 * span, 1), y1),
+                jnp.where(even, y2, pltpu.roll(y3, span, 1)),
+                jnp.where(even, pltpu.roll(y2, 3 * span, 1), y3),
+            ]
+            for i in range(4):
+                a = (block * tiles + tile) * 4 + i
+                turned[pl.ds(a, widen * group, stride=inputs), :] = swapped[i]
+
+    def cast(part):
         @pl.loop(0, widen)
         def one(d):
             rows = pl.ds(pl.multiple_of(d * (group * inputs), group * inputs), group * inputs)
-            spec[d, parity] = turned[rows, :].astype(jnp.bfloat16)
+            spec[d, part] = turned[rows, :].astype(jnp.bfloat16)
 
     onward_copies, own_copies = [], []
 
@@ -230,26 +241,42 @@
         pass_on(out_ref.at[t, flipped(w, i), parity], parity, i)
         start_next(limit)
 
+    handled = 0
+
+    def handle_some(count, limit):
+        nonlocal handled
+        for _ in range(count):
+            handle(handled, limit)
+            handled += 1
+
+    for first in range(span, frames, STEP):
+        fir_later(first)
+    load_table.wait()
+
     @pl.loop(0, blocks)
-    def dft_even(block):
-        dft(0, block)
+    def dft_late(block):
+        dft(block)
 
     cast(0)
     for _ in range(WINDOW):
         start_next(len(order))
     own(0)
-    handled = 0
-    for block in range(blocks):
-        dft(1, block)
-        handle(handled, len(order))
-        handled += 1
+    for first in range(STEP, span, STEP):
+        fir_later(first)
+    handle_some(3, len(order))
+    fir_first()
+    handle_some(2, len(order))
+
+    @pl.loop(0, blocks)
+    def dft_early(block):
+        dft(block)
+
+    handle_some(2, len(order))
     cast(1)
     own(1)
     while len(started) < handled + WINDOW:
         start_next(len(sequence))
-    while handled < len(sequence):
-        handle(handled, len(sequence))
-        handled += 1
+    handle_some(len(sequence) - handled, len(sequence))
 
     for copy in own_copies:
         copy.wait()
@@ -285,7 +312,8 @@
             pltpu.VMEM(halo_shape, jnp.bfloat16),
             pltpu.VMEM(halo_shape, jnp.float32),
             pltpu.VMEM(table.shape, jnp.bfloat16),
-            pltpu.VMEM((2 * half // LANES, inputs * frames, LANES), jnp.float32),
+            pltpu.VMEM((2 * half // LANES, inputs * frames // 2, LANES), jnp.float32),
+            pltpu.VMEM((2, half, COLUMNS), jnp.float32),
             pltpu.VMEM((half // 2 * inputs, LANES), jnp.float32),
             pltpu.VMEM((widen,) + block, jnp.bfloat16),
             pltpu.SemaphoreType.DMA(()),
@@ -317,55 +345,60 @@
 
 
 def gram_rows(full, inputs, channels, norm):
-    ranks, widen, _, _, width = full.shape
+    ranks, widen, parts, _, width = full.shape
     total = widen * inputs
     own = total // ranks
     step = SUBLANES
+    pairs = step // 2
+    span = width // 4
     first = (lax.axis_index("tm") * (own // inputs)).astype(jnp.int32).reshape(1)
-    pairs = step // 2
-
-    def kernel(first_ref, even_ref, odd_ref, out_ref):
+    pieces = [(t, part) for t in range(ranks) for part in range(parts)]
+
+    def kernel(first_ref, ref, out_ref, turned):
         own_from = first_ref[0]
         lane = lax.broadcasted_iota(jnp.int32, (own, width), 1)
-        sign = jnp.where(lane < width // 2, norm, -norm)
-        for k in range(step):
-            ref = (even_ref, odd_ref)[k % 2]
-            at = pl.ds(k // 2 * inputs, inputs)
+        real = (lane // span) % 2 == 0
+        masks = [jnp.where(lane // (2 * span) == parity, norm, 0.0) for parity in range(2)]
+        for j in range(pairs):
+            at = pl.ds(j * inputs, inputs)
             whole = jnp.concatenate(
-                [ref[t, :, 0, at, :].reshape(total, width) for t in range(ranks)], axis=1
+                [ref[t, :, part, at, :].reshape(total, width) for t, part in pieces], axis=1
             )
-            mine = [
-                ref[t, pl.ds(own_from, own // inputs), 0, at, :].reshape(own, width)
-                for t in range(ranks)
-            ]
-            rotated = [
-                (pltpu.roll(x.astype(jnp.float32), width // 2, 1) * sign).astype(jnp.bfloat16)
-                for x in mine
-            ]
-            scaled = [(x.astype(jnp.float32) * norm).astype(jnp.bfloat16) for x in mine]
-            left = jnp.concatenate(
-                [jnp.concatenate(scaled, axis=1), jnp.concatenate(rotated, axis=1)], axis=0
-            )
+            rows = [[] for _ in range(4)]
+            for t, part in pieces:
+                x = ref[t, pl.ds(own_from, own // inputs), part, at, :].reshape(own, width)
+                x = x.astype(jnp.float32)
+                turn = jnp.where(real, pltpu.roll(x, 3 * span, 1), -pltpu.roll(x, span, 1))
+                for parity in range(2):
+                    rows[2 * parity].append((x * masks[parity]).astype(jnp.bfloat16))
+                    rows[2 * parity + 1].append((turn * masks[parity]).astype(jnp.bfloat16))
+            left = jnp.concatenate([jnp.concatenate(row, axis=1) for row in rows], axis=0)
             gram = lax.dot_general(
                 left, whole, (((1,), (1,)), ((), ())), preferred_element_type=jnp.float32
             )
-            out_ref[:, 0, k, :] = gram[:own]
-            out_ref[:, 1, k, :] = gram[own:]
-
-    block = (ranks, widen, 1, pairs * inputs, width)
+            for parity in range(2):
+                for r in range(2):
+                    top = (2 * parity + r) * own
+                    for l in range(total // LANES):
+                        turned[l, pl.ds(r * step + 2 * j + parity, own, stride=2 * step), :] = (
+                            gram[top : top + own, l * LANES : (l + 1) * LANES]
+                        )
+        for l in range(total // LANES):
+            out_ref[:, :, :, l * LANES : (l + 1) * LANES] = turned[l].reshape(own, 2, step, LANES)
+
     return pl.pallas_call(
         kernel,
         grid=(channels // step,),
         out_shape=jax.ShapeDtypeStruct((own, 2, channels, total), jnp.float32),
         in_specs=[
             pl.BlockSpec(memory_space=pltpu.SMEM),
-            pl.BlockSpec(block, lambda i: (0, 0, 0, i, 0)),
-            pl.BlockSpec(block, lambda i: (0, 0, 1, i, 0)),
+            pl.BlockSpec((ranks, widen, parts, pairs * inputs, width), lambda i: (0, 0, 0, i, 0)),
         ],
         out_specs=pl.BlockSpec((own, 2, step, total), lambda i: (0, 0, i, 0)),
+        scratch_shapes=[pltpu.VMEM((total // LANES, own * 2 * step, LANES), jnp.float32)],
         compiler_params=pltpu.CompilerParams(vmem_limit_bytes=VMEM_BYTES),
         name="gram",
-    )(first, full, full)
+    )(first, full)
 
 
 def solution(mesh):

time: 94.3 us -> 86.4 us (0.916)
  the two profiles are of different devices: /device:TPU:17 before, /device:TPU:19 now
where the time goes in v3:
time: 86.4 us; the launch traced here: 86.2 us
  Pallas kernels  86.2 us (100%)
    pallas_call x1, Pallas kernels, exchanged_spectra(): pl.pallas_call(functools.partial(spectra_kernel, widen, ranks), out_shape...  77.1 us
    pallas_call x1, Pallas kernels, gram_rows(): pl.pallas_call(kernel, grid=(channels // step,), out_shape=jax.ShapeDtype...  9.07 us

profile of v3, /device:TPU:19, one launch (start us, length us, event | category | flops | bytes accessed | tf_op | source)
XLA Modules:
  0.0 86.2 jit_solution(10221955920084006601)
XLA Ops:
  0.0 77.1 %spectra_exchange.1.ref = bf16[2,16,2,256,128]{4,3,2,1,0:T(8,128)(2,1)} custom-call(s32[16,65536]{1,0:T(8,128)} %volt_ref.1, s32[16,1024]{1,0:T(8,128)} %taps_ref.1, bf16[2,512,1536]{2,1,0:T(8,128)(2,1)} %constant.8.clone.table_hbm), custom_call_target="tpu_custom_call" | custom-call | tf_op jit(solution)/shard_map/spectra_exchange/pallas_call | solution.py:301
  77.2 9.1 %gram.1 = f32[128,2,32,256]{3,2,1,0:T(8,128)} custom-call(s32[1]{0:T(128)} %bitcast.first_ref, bf16[2,16,2,256,128]{4,3,2,1,0:T(8,128)(2,1)} %spectra_exchange.1.ref), custom_call_target="tpu_custom_call" | custom-call | tf_op jit(solution)/shard_map/gram/pallas_call | solution.py:389

commit v4 on v3

--- a/solution.py
+++ b/solution.py
@@ -15,7 +15,8 @@
 LANES = 128
 STEP = 16
 COLUMNS = 256
-WINDOW = 8
+WINDOW = 12
+CARRIER = jnp.bfloat16
 VMEM_BYTES = 56 * 1024 * 1024
 
 
@@ -46,11 +47,10 @@
 
 def send_order(widen):
     far = [i for i in range(widen // 2, widen)]
-    near = [i for i in range(2, widen // 2)]
-    order = [1]
-    while far or near:
-        order += far[:2] + near[:1]
-        far, near = far[2:], near[1:]
+    near = [i for i in range(1, widen // 2)]
+    order = []
+    for i, other in enumerate(far):
+        order += near[i : i + 1] + [other]
     return order
 
 
@@ -352,53 +352,71 @@
     pairs = step // 2
     span = width // 4
     first = (lax.axis_index("tm") * (own // inputs)).astype(jnp.int32).reshape(1)
-    pieces = [(t, part) for t in range(ranks) for part in range(parts)]
-
-    def kernel(first_ref, ref, out_ref, turned):
+
+    tiles = total // LANES
+    sides = own // inputs
+
+    def kernel(first_ref, ref, out_ref):
         own_from = first_ref[0]
-        lane = lax.broadcasted_iota(jnp.int32, (own, width), 1)
-        real = (lane // span) % 2 == 0
-        masks = [jnp.where(lane // (2 * span) == parity, norm, 0.0) for parity in range(2)]
+        flat = out_ref.reshape(own * 2 * tiles * step, LANES)
+
+        def picked(parity, first, second, lower):
+            if parity:
+                first = pltpu.roll(first, 2 * span, 1)
+            else:
+                second = pltpu.roll(second, 2 * span, 1)
+            return jnp.where(lower, first, second)
+
+        def lanes(rows):
+            return lax.broadcasted_iota(jnp.int32, (rows, width), 1)
+
         for j in range(pairs):
             at = pl.ds(j * inputs, inputs)
-            whole = jnp.concatenate(
-                [ref[t, :, part, at, :].reshape(total, width) for t, part in pieces], axis=1
-            )
-            rows = [[] for _ in range(4)]
-            for t, part in pieces:
-                x = ref[t, pl.ds(own_from, own // inputs), part, at, :].reshape(own, width)
-                x = x.astype(jnp.float32)
-                turn = jnp.where(real, pltpu.roll(x, 3 * span, 1), -pltpu.roll(x, span, 1))
-                for parity in range(2):
-                    rows[2 * parity].append((x * masks[parity]).astype(jnp.bfloat16))
-                    rows[2 * parity + 1].append((turn * masks[parity]).astype(jnp.bfloat16))
-            left = jnp.concatenate([jnp.concatenate(row, axis=1) for row in rows], axis=0)
-            gram = lax.dot_general(
-                left, whole, (((1,), (1,)), ((), ())), preferred_element_type=jnp.float32
-            )
             for parity in range(2):
+                whole, mine, turned = [], [], []
+                for t in range(ranks):
+                    halves = [
+                        ref[t, :, h, at, :].reshape(total, width).astype(CARRIER) for h in range(2)
+                    ]
+                    whole.append(picked(parity, *halves, lanes(total) < 2 * span))
+                    halves = [
+                        ref[t, pl.ds(own_from, sides), h, at, :].reshape(own, width)
+                        .astype(jnp.float32)
+                        for h in range(2)
+                    ]
+                    x = picked(parity, *halves, lanes(own) < 2 * span)
+                    real = (lanes(own) // span) % 2 == 0
+                    mine.append(x)
+                    turned.append(
+                        jnp.where(real, pltpu.roll(x, 3 * span, 1), -pltpu.roll(x, span, 1))
+                    )
+                left = jnp.concatenate(
+                    [jnp.concatenate(mine, axis=1), jnp.concatenate(turned, axis=1)], axis=0
+                ).astype(jnp.bfloat16)
+                right = jnp.concatenate(whole, axis=1).astype(jnp.bfloat16)
+                gram = norm * lax.dot_general(
+                    left, right, (((1,), (1,)), ((), ())), preferred_element_type=jnp.float32
+                )
                 for r in range(2):
-                    top = (2 * parity + r) * own
-                    for l in range(total // LANES):
-                        turned[l, pl.ds(r * step + 2 * j + parity, own, stride=2 * step), :] = (
-                            gram[top : top + own, l * LANES : (l + 1) * LANES]
-                        )
-        for l in range(total // LANES):
-            out_ref[:, :, :, l * LANES : (l + 1) * LANES] = turned[l].reshape(own, 2, step, LANES)
-
-    return pl.pallas_call(
+                    for l in range(tiles):
+                        base = (r * tiles + l) * step + 2 * j + parity
+                        flat[pl.ds(base, own, stride=2 * tiles * step), :] = gram[
+                            r * own : (r + 1) * own, l * LANES : (l + 1) * LANES
+                        ]
+
+    tiled = pl.pallas_call(
         kernel,
         grid=(channels // step,),
-        out_shape=jax.ShapeDtypeStruct((own, 2, channels, total), jnp.float32),
+        out_shape=jax.ShapeDtypeStruct((own, 2, channels // step, tiles, step, LANES), jnp.float32),
         in_specs=[
             pl.BlockSpec(memory_space=pltpu.SMEM),
             pl.BlockSpec((ranks, widen, parts, pairs * inputs, width), lambda i: (0, 0, 0, i, 0)),
         ],
-        out_specs=pl.BlockSpec((own, 2, step, total), lambda i: (0, 0, i, 0)),
-        scratch_shapes=[pltpu.VMEM((total // LANES, own * 2 * step, LANES), jnp.float32)],
+        out_specs=pl.BlockSpec((own, 2, 1, tiles, step, LANES), lambda i: (0, 0, i, 0, 0, 0)),
         compiler_params=pltpu.CompilerParams(vmem_limit_bytes=VMEM_BYTES),
         name="gram",
     )(first, full)
+    return jnp.swapaxes(tiled, 3, 4).reshape(own, 2, channels, total)
 
 
 def solution(mesh):

time: 86.4 us -> 85.7 us (level)
  the two profiles are of different devices: /device:TPU:19 before, /device:TPU:0 now
where the time goes in v4:
time: 85.7 us; the launch traced here: 85.5 us
  Pallas kernels  85.5 us (100%)
    pallas_call x1, Pallas kernels, exchanged_spectra(): pl.pallas_call(functools.partial(spectra_kernel, widen, ranks), out_shape...  73 us
    pallas_call x1, Pallas kernels, gram_rows(): pl.pallas_call(kernel, grid=(channels // step,), out_shape=jax.ShapeDtype...  12.5 us

profile of v4, /device:TPU:0, one launch (start us, length us, event | category | flops | bytes accessed | tf_op | source)
XLA Modules:
  0.0 85.5 jit_solution(6654314347687932314)
XLA Ops:
  0.0 73.0 %spectra_exchange.1.ref = bf16[2,16,2,256,128]{4,3,2,1,0:T(8,128)(2,1)} custom-call(s32[16,65536]{1,0:T(8,128)} %volt_ref.1, s32[16,1024]{1,0:T(8,128)} %taps_ref.1, bf16[2,512,1536]{2,1,0:T(8,128)(2,1)} %constant.8.clone.table_hbm), custom_call_target="tpu_custom_call" | custom-call | tf_op jit(solution)/shard_map/spectra_exchange/pallas_call | solution.py:301
  73.1 12.5 %gram.1 = f32[128,2,4,2,8,128]{5,4,3,2,1,0:T(8,128)} custom-call(s32[1]{0:T(128)} %bitcast.first_ref, bf16[2,16,2,256,128]{4,3,2,1,0:T(8,128)(2,1)} %spectra_exchange.1.ref), custom_call_target="tpu_custom_call" | custom-call | tf_op jit(solution)/shard_map/gram/pallas_call | solution.py:407

commit v5 on v4

--- a/solution.py
+++ b/solution.py
@@ -15,8 +15,7 @@
 LANES = 128
 STEP = 16
 COLUMNS = 256
-WINDOW = 12
-CARRIER = jnp.bfloat16
+WINDOW = 16
 VMEM_BYTES = 56 * 1024 * 1024
 
 
@@ -55,9 +54,9 @@
 
 
 def spectra_kernel(
-    widen, ranks, volt_ref, taps_ref, table_hbm, out_ref,
-    tail, halo, before, table_ref, folded, product, turned, spec,
-    table_sem, own_sem, halo_sems, send_wide, recv_wide, send_tm, recv_tm,
+    widen, ranks, volt_hbm, taps_ref, table_hbm, out_ref,
+    volt_ref, tail, halo, before, table_ref, folded, product, turned, spec,
+    volt_sems, table_sem, own_sem, halo_sems, send_wide, recv_wide, send_tm, recv_tm,
 ):
     w = lax.axis_index("wide")
     t = lax.axis_index("tm")
@@ -77,22 +76,20 @@
         pl.semaphore_signal(
             barrier, inc=1, device_id=(w, lax.rem(t + r, ranks)), device_id_type=MESH
         )
+    border = (frames // 2 - lags) * length
+    loads = []
+    for i, (start, size) in enumerate([(border, frames * length - border), (0, border)]):
+        at = pl.ds(start, size)
+        load = pltpu.make_async_copy(volt_hbm.at[:, at], volt_ref.at[:, at], volt_sems.at[i])
+        load.start()
+        loads.append(load)
     load_table = pltpu.make_async_copy(table_hbm, table_ref, table_sem)
     load_table.start()
-    from_frame = (frames - lags + 1) * length
-    for p in range(lags - 1):
-        at = pl.ds(p * length, length)
-        tail[:, at] = volt_ref[:, pl.ds(from_frame + p * length, length)].astype(jnp.bfloat16)
-    pl.semaphore_wait(barrier, len(order) + ranks - 1)
 
     halo_copy = pltpu.make_async_remote_copy(
         src_ref=tail, dst_ref=halo, send_sem=halo_sems.at[0], recv_sem=halo_sems.at[1],
         device_id=(w, lax.rem(t + 1, ranks)), device_id_type=MESH,
     )
-
-    @pl.when(t < ranks - 1)
-    def send_halo():
-        halo_copy.start()
 
     span = frames // 2
 
@@ -249,7 +246,19 @@
             handle(handled, limit)
             handled += 1
 
-    for first in range(span, frames, STEP):
+    loads[0].wait()
+    from_frame = (frames - lags + 1) * length
+    for p in range(lags - 1):
+        at = pl.ds(p * length, length)
+        tail[:, at] = volt_ref[:, pl.ds(from_frame + p * length, length)].astype(jnp.bfloat16)
+    fir_later(span)
+    pl.semaphore_wait(barrier, len(order) + ranks - 1)
+
+    @pl.when(t < ranks - 1)
+    def send_halo():
+        halo_copy.start()
+
+    for first in range(span + STEP, frames, STEP):
         fir_later(first)
     load_table.wait()
 
@@ -261,6 +270,7 @@
     for _ in range(WINDOW):
         start_next(len(order))
     own(0)
+    loads[1].wait()
     for first in range(STEP, span, STEP):
         fir_later(first)
     handle_some(3, len(order))
@@ -302,12 +312,13 @@
         functools.partial(spectra_kernel, widen, ranks),
         out_shape=jax.ShapeDtypeStruct((ranks, widen) + block, jnp.bfloat16),
         in_specs=[
-            pl.BlockSpec(memory_space=pltpu.VMEM),
+            pl.BlockSpec(memory_space=pl.ANY),
             pl.BlockSpec(memory_space=pltpu.VMEM),
             pl.BlockSpec(memory_space=pl.ANY),
         ],
         out_specs=pl.BlockSpec(memory_space=pl.ANY),
         scratch_shapes=[
+            pltpu.VMEM(voltages.shape, jnp.int32),
             pltpu.VMEM(halo_shape, jnp.bfloat16),
             pltpu.VMEM(halo_shape, jnp.bfloat16),
             pltpu.VMEM(halo_shape, jnp.float32),
@@ -316,6 +327,7 @@
             pltpu.VMEM((2, half, COLUMNS), jnp.float32),
             pltpu.VMEM((half // 2 * inputs, LANES), jnp.float32),
             pltpu.VMEM((widen,) + block, jnp.bfloat16),
+            pltpu.SemaphoreType.DMA((2,)),
             pltpu.SemaphoreType.DMA(()),
             pltpu.SemaphoreType.DMA((2,)),
             pltpu.SemaphoreType.DMA((2,)),
@@ -355,53 +367,58 @@
 
     tiles = total // LANES
     sides = own // inputs
+    pieces = [(t, h) for t in range(ranks) for h in range(parts)]
 
     def kernel(first_ref, ref, out_ref):
         own_from = first_ref[0]
         flat = out_ref.reshape(own * 2 * tiles * step, LANES)
 
-        def picked(parity, first, second, lower):
-            if parity:
-                first = pltpu.roll(first, 2 * span, 1)
-            else:
-                second = pltpu.roll(second, 2 * span, 1)
-            return jnp.where(lower, first, second)
-
-        def lanes(rows):
-            return lax.broadcasted_iota(jnp.int32, (rows, width), 1)
+        source = lax.broadcasted_iota(jnp.int32, (width, 2 * width), 0)
+        target = lax.broadcasted_iota(jnp.int32, (width, 2 * width), 1)
+        lane = target % width
+        partner = jnp.where((lane // span) % 2 == 0, lane + span, lane - span)
+        swap = jnp.where((lane // span) % 2 == 0, 1.0, -1.0)
+        swap = jnp.where(
+            (source == partner) & (lane // (2 * span) == target // width), swap, 0.0
+        ).astype(jnp.bfloat16)
+        lane = lax.broadcasted_iota(jnp.int32, (own, width), 1)
+        masks = [
+            jnp.where(lane // (2 * span) == parity, 1.0, 0.0).astype(jnp.bfloat16)
+            for parity in range(2)
+        ]
 
         for j in range(pairs):
             at = pl.ds(j * inputs, inputs)
+            whole = jnp.concatenate(
+                [ref[t, :, h, at, :].reshape(total, width) for t, h in pieces], axis=1
+            )
+            mine = [
+                ref[t, pl.ds(own_from, sides), h, at, :].reshape(own, width) for t, h in pieces
+            ]
+            swapped = lax.dot_general(
+                jnp.concatenate(mine, axis=0), swap, (((1,), (0,)), ((), ())),
+                preferred_element_type=jnp.float32,
+            ).astype(jnp.bfloat16)
+            left = []
             for parity in range(2):
-                whole, mine, turned = [], [], []
-                for t in range(ranks):
-                    halves = [
-                        ref[t, :, h, at, :].reshape(total, width).astype(CARRIER) for h in range(2)
-                    ]
-                    whole.append(picked(parity, *halves, lanes(total) < 2 * span))
-                    halves = [
-                        ref[t, pl.ds(own_from, sides), h, at, :].reshape(own, width)
-                        .astype(jnp.float32)
-                        for h in range(2)
-                    ]
-                    x = picked(parity, *halves, lanes(own) < 2 * span)
-                    real = (lanes(own) // span) % 2 == 0
-                    mine.append(x)
-                    turned.append(
-                        jnp.where(real, pltpu.roll(x, 3 * span, 1), -pltpu.roll(x, span, 1))
+                left.append(jnp.concatenate([x * masks[parity] for x in mine], axis=1))
+                columns = swapped[:, parity * width : (parity + 1) * width]
+                left.append(
+                    jnp.concatenate(
+                        [columns[i * own : (i + 1) * own] for i in range(len(pieces))], axis=1
                     )
-                left = jnp.concatenate(
-                    [jnp.concatenate(mine, axis=1), jnp.concatenate(turned, axis=1)], axis=0
-                ).astype(jnp.bfloat16)
-                right = jnp.concatenate(whole, axis=1).astype(jnp.bfloat16)
-                gram = norm * lax.dot_general(
-                    left, right, (((1,), (1,)), ((), ())), preferred_element_type=jnp.float32
                 )
+            gram = norm * lax.dot_general(
+                jnp.concatenate(left, axis=0), whole, (((1,), (1,)), ((), ())),
+                preferred_element_type=jnp.float32,
+            )
+            for parity in range(2):
                 for r in range(2):
+                    top = (2 * parity + r) * own
                     for l in range(tiles):
                         base = (r * tiles + l) * step + 2 * j + parity
                         flat[pl.ds(base, own, stride=2 * tiles * step), :] = gram[
-                            r * own : (r + 1) * own, l * LANES : (l + 1) * LANES
+                            top : top + own, l * LANES : (l + 1) * LANES
                         ]
 
     tiled = pl.pallas_call(

time: 85.7 us -> 84.7 us (0.988)
  Pallas kernels: 85.5 us -> 84.5 us
    pallas_call x1, Pallas kernels: 12.5 us -> 10.7 us  [gram_rows(): pl.pallas_call(kernel, grid=(channels // step,), out_shape=jax.ShapeDtype...]
where the time goes in v5:
time: 84.7 us; the launch traced here: 84.5 us
  Pallas kernels  84.5 us (100%)
    pallas_call x1, Pallas kernels, exchanged_spectra(): pl.pallas_call(functools.partial(spectra_kernel, widen, ranks), out_shape...  73.8 us
    pallas_call x1, Pallas kernels, gram_rows(): pl.pallas_call(kernel, grid=(channels // step,), out_shape=jax.ShapeDtype...  10.7 us

profile of v5, /device:TPU:0, one launch (start us, length us, event | category | flops | bytes accessed | tf_op | source)
XLA Modules:
  0.0 84.5 jit_solution(13817224663319400331)
XLA Ops:
  0.0 73.8 %spectra_exchange.1.ref = bf16[2,16,2,256,128]{4,3,2,1,0:T(8,128)(2,1)} custom-call(s32[16,65536]{1,0:T(8,128)} %volt_hbm.1, s32[16,1024]{1,0:T(8,128)} %taps_ref.1, bf16[2,512,1536]{2,1,0:T(8,128)(2,1)} %constant.8.clone.table_hbm), custom_call_target="tpu_custom_call" | custom-call | tf_op jit(solution)/shard_map/spectra_exchange/pallas_call | solution.py:311
  73.8 10.7 %gram.1 = f32[128,2,4,2,8,128]{5,4,3,2,1,0:T(8,128)} custom-call(s32[1]{0:T(128)} %bitcast.first_ref, bf16[2,16,2,256,128]{4,3,2,1,0:T(8,128)(2,1)} %spectra_exchange.1.ref), custom_call_target="tpu_custom_call" | custom-call | tf_op jit(solution)/shard_map/gram/pallas_call | solution.py:424

commit v6 on v5

--- a/solution.py
+++ b/solution.py
@@ -51,6 +51,21 @@
     for i, other in enumerate(far):
         order += near[i : i + 1] + [other]
     return order
+
+
+def exchanged_sublanes(rows):
+    axis = rows[0].ndim - 2
+    sublane = lax.broadcasted_iota(jnp.int32, rows[0].shape, axis)
+    for d in (4, 2, 1):
+        low = (sublane // d) % 2 == 0
+        new = list(rows)
+        for i in range(SUBLANES):
+            if i & d == 0:
+                x, y = rows[i], rows[i + d]
+                new[i] = jnp.where(low, x, pltpu.roll(y, d, axis))
+                new[i + d] = jnp.where(low, pltpu.roll(x, SUBLANES - d, axis), y)
+        rows = new
+    return rows
 
 
 def spectra_kernel(
@@ -108,9 +123,11 @@
                 total = term if total is None else total + term
             sums.append(total)
         for number, value in enumerate((sums[0] + sums[1], sums[0] - sums[1])):
-            for i in range(STEP):
-                at = pl.ds(g * (SUBLANES * span) + first % span + i, SUBLANES, stride=span)
-                folded[number * chunks + c, at, :] = value[i]
+            for b in range(0, STEP, SUBLANES):
+                lines = exchanged_sublanes([value[b + i] for i in range(SUBLANES)])
+                for i in range(SUBLANES):
+                    at = pl.ds(first % span + b, SUBLANES)
+                    folded[number * chunks + c, g * SUBLANES + i, at, :] = lines[i]
 
     def fir_later(first):
         @pl.loop(0, groups * chunks)
@@ -149,11 +166,11 @@
     even = (lane_at // span) % 2 == 0
 
     def dft(block):
-        rows = pl.ds(pl.multiple_of(block * COLUMNS, COLUMNS), COLUMNS)
+        rows = pl.ds(block * SUBLANES, SUBLANES)
         for parity in range(2):
             high, low = [], []
             for c in range(chunks):
-                value = folded[parity * chunks + c, rows, :]
+                value = folded[parity * chunks + c, rows].reshape(COLUMNS, LANES)
                 top = value.astype(jnp.bfloat16)
                 high.append(top)
                 low.append((value - top.astype(jnp.float32)).astype(jnp.bfloat16))
@@ -162,6 +179,7 @@
                 table_ref[parity], operand, (((1,), (1,)), ((), ())),
                 preferred_element_type=jnp.float32,
             )
+        lines = []
         for tile in range(tiles):
             parts = []
             for parity in range(2):
@@ -174,21 +192,22 @@
             y2 = jnp.where(lower, pltpu.roll(x0, 2 * span, 1), x2)
             y1 = jnp.where(lower, x1, pltpu.roll(x3, 2 * span, 1))
             y3 = jnp.where(lower, pltpu.roll(x1, 2 * span, 1), x3)
-            swapped = [
+            lines += [
                 jnp.where(even, y0, pltpu.roll(y1, span, 1)),
                 jnp.where(even, pltpu.roll(y0, 3 * span, 1), y1),
                 jnp.where(even, y2, pltpu.roll(y3, span, 1)),
                 jnp.where(even, pltpu.roll(y2, 3 * span, 1), y3),
             ]
-            for i in range(4):
-                a = (block * tiles + tile) * 4 + i
-                turned[pl.ds(a, widen * group, stride=inputs), :] = swapped[i]
+        lines = [x.reshape(widen * group // SUBLANES, SUBLANES, LANES) for x in lines]
+        lines = exchanged_sublanes(lines)
+        for j in range(SUBLANES):
+            turned[:, j, block] = lines[j]
 
     def cast(part):
         @pl.loop(0, widen)
         def one(d):
-            rows = pl.ds(pl.multiple_of(d * (group * inputs), group * inputs), group * inputs)
-            spec[d, part] = turned[rows, :].astype(jnp.bfloat16)
+            rows = pl.ds(d * (group // SUBLANES), group // SUBLANES)
+            spec[d, part] = turned[rows].reshape(group * inputs, LANES).astype(jnp.bfloat16)
 
     onward_copies, own_copies = [], []
 
@@ -323,9 +342,11 @@
             pltpu.VMEM(halo_shape, jnp.bfloat16),
             pltpu.VMEM(halo_shape, jnp.float32),
             pltpu.VMEM(table.shape, jnp.bfloat16),
-            pltpu.VMEM((2 * half // LANES, inputs * frames // 2, LANES), jnp.float32),
+            pltpu.VMEM((2 * half // LANES, inputs, frames // 2, LANES), jnp.float32),
             pltpu.VMEM((2, half, COLUMNS), jnp.float32),
-            pltpu.VMEM((half // 2 * inputs, LANES), jnp.float32),
+            pltpu.VMEM(
+                (half // 2 // SUBLANES, SUBLANES, inputs // SUBLANES, SUBLANES, LANES), jnp.float32
+            ),
             pltpu.VMEM((widen,) + block, jnp.bfloat16),
             pltpu.SemaphoreType.DMA((2,)),
             pltpu.SemaphoreType.DMA(()),
@@ -369,9 +390,8 @@
     sides = own // inputs
     pieces = [(t, h) for t in range(ranks) for h in range(parts)]
 
-    def kernel(first_ref, ref, out_ref):
+    def kernel(first_ref, ref, out_ref, grams):
         own_from = first_ref[0]
-        flat = out_ref.reshape(own * 2 * tiles * step, LANES)
 
         source = lax.broadcasted_iota(jnp.int32, (width, 2 * width), 0)
         target = lax.broadcasted_iota(jnp.int32, (width, 2 * width), 1)
@@ -415,25 +435,33 @@
             for parity in range(2):
                 for r in range(2):
                     top = (2 * parity + r) * own
-                    for l in range(tiles):
-                        base = (r * tiles + l) * step + 2 * j + parity
-                        flat[pl.ds(base, own, stride=2 * tiles * step), :] = gram[
-                            top : top + own, l * LANES : (l + 1) * LANES
-                        ]
-
-    tiled = pl.pallas_call(
+                    grams[2 * j + parity, r] = gram[top : top + own]
+
+        for r in range(2):
+            for l in range(tiles):
+                at = pl.ds(l * LANES, LANES)
+                lines = exchanged_sublanes(
+                    [grams[k, r, :, at].reshape(own // SUBLANES, SUBLANES, LANES) for k in range(step)]
+                )
+                for i in range(SUBLANES):
+                    out_ref[:, i, r, :, at] = lines[i]
+
+    rows = pl.pallas_call(
         kernel,
         grid=(channels // step,),
-        out_shape=jax.ShapeDtypeStruct((own, 2, channels // step, tiles, step, LANES), jnp.float32),
+        out_shape=jax.ShapeDtypeStruct((own // SUBLANES, SUBLANES, 2, channels, total), jnp.float32),
         in_specs=[
             pl.BlockSpec(memory_space=pltpu.SMEM),
             pl.BlockSpec((ranks, widen, parts, pairs * inputs, width), lambda i: (0, 0, 0, i, 0)),
         ],
-        out_specs=pl.BlockSpec((own, 2, 1, tiles, step, LANES), lambda i: (0, 0, i, 0, 0, 0)),
+        out_specs=pl.BlockSpec(
+            (own // SUBLANES, SUBLANES, 2, step, total), lambda i: (0, 0, 0, i, 0)
+        ),
+        scratch_shapes=[pltpu.VMEM((step, 2, own, total), jnp.float32)],
         compiler_params=pltpu.CompilerParams(vmem_limit_bytes=VMEM_BYTES),
         name="gram",
     )(first, full)
-    return jnp.swapaxes(tiled, 3, 4).reshape(own, 2, channels, total)
+    return rows.reshape(own, 2, channels, total)
 
 
 def solution(mesh):

time: 84.7 us -> 82.2 us (0.970)
  Pallas kernels: 84.5 us -> 81.9 us
    pallas_call x1, Pallas kernels: 10.7 us -> 8.72 us  [gram_rows(): pl.pallas_call(kernel, grid=(channels // step,), out_shape=jax.ShapeDtype...]
where the time goes in v6:
time: 82.2 us; the launch traced here: 82 us
  Pallas kernels  81.9 us (100%)
    pallas_call x1, Pallas kernels, exchanged_spectra(): pl.pallas_call(functools.partial(spectra_kernel, widen, ranks), out_shape...  73.2 us
    pallas_call x1, Pallas kernels, gram_rows(): pl.pallas_call(kernel, grid=(channels // step,), out_shape=jax.ShapeDtype...  8.72 us

profile of v6, /device:TPU:0, one launch (start us, length us, event | category | flops | bytes accessed | tf_op | source)
XLA Modules:
  0.0 82.0 jit_solution(13719855453851816865)
XLA Ops:
  0.0 73.2 %spectra_exchange.1.ref = bf16[2,16,2,256,128]{4,3,2,1,0:T(8,128)(2,1)} custom-call(s32[16,65536]{1,0:T(8,128)} %volt_hbm.1, s32[16,1024]{1,0:T(8,128)} %taps_ref.1, bf16[2,512,1536]{2,1,0:T(8,128)(2,1)} %constant.8.clone.table_hbm), custom_call_target="tpu_custom_call" | custom-call | tf_op jit(solution)/shard_map/spectra_exchange/pallas_call | solution.py:330
  73.2 8.7 %gram.1 = f32[16,8,2,32,256]{4,3,2,1,0:T(8,128)} custom-call(s32[1]{0:T(128)} %bitcast.first_ref, bf16[2,16,2,256,128]{4,3,2,1,0:T(8,128)(2,1)} %spectra_exchange.1.ref), custom_call_target="tpu_custom_call" | custom-call | tf_op jit(solution)/shard_map/gram/pallas_call | solution.py:449
